TPU v7x, 256 devices: a whole 4x4x8 slice. The times are simulated.
256 devices in a mesh: replica: 16 (over x_hi, z), fsdp: 16 (over y, x_lo, core).
Axes of the slice: x: 4 (x_hi: 2, x_lo: 2; x = x_hi * 2 + x_lo), y: 4, z: 8, core: 2. Of those that a mesh axis runs over, the one named last changes fastest.
Arguments:
- local_params: bfloat16 [16, 2048, 8192], P('replica', 'fsdp'), may hold values from -6 to 6
- global_params: bfloat16 [2048, 8192], P('fsdp'), may hold values from -6 to 6
- momentum: float32 [2048, 2048], P('fsdp'), may hold values from -4 to 4
- kept: int32 [32], replicated, may hold values from 0 to 31, as said below
Outputs:
- new_params: bfloat16 [2048, 8192], replicated
- new_momentum: float32 [2048, 2048], P('fsdp')
Inputs may be any that keep to these rules, and one draw needn't show every extreme that they name: `kept`: a permutation of 0 to 31.
All inputs are finite; a program needn't handle non-finite values.
Results may differ from a plain program's by a relative error of at most 0.017.
Values may be sent and summed in bfloat16 or wider, within the bound.
A program may use at most 192 MiB of HBM per device.

v0:
```python
import jax
import jax.numpy as jnp
from jax import lax
from jax.sharding import PartitionSpec as P

BLOCK = 128
KEEP = 32


def make_basis(kept):
    freq = kept.astype(jnp.float32)[:, None]
    place = jnp.arange(BLOCK).astype(jnp.float32)[None, :]
    scale = jnp.where(kept[:, None] == 0, jnp.sqrt(1.0 / BLOCK), jnp.sqrt(2.0 / BLOCK)).astype(
        jnp.float32
    )
    return scale * jnp.cos(jnp.pi * (2.0 * place + 1.0) * freq / (2.0 * BLOCK))


def outer_update(total, momentum, glob, basis, replicas):
    count = glob.shape[0]
    width = glob.shape[1]
    nblocks = width // BLOCK
    mean = (total / replicas).reshape(count, nblocks, KEEP)
    new_mom = 0.9 * momentum.reshape(count, nblocks, KEEP) + mean
    step = mean + 0.9 * new_mom
    update = jnp.einsum("rbj,jn->rbn", step, basis, precision=lax.Precision.HIGHEST).reshape(
        count, width
    )
    new_rows = (glob - 0.7 * update).astype(jnp.bfloat16)
    return (new_mom.reshape(count, nblocks * KEEP), new_rows)


def on_device(local_params, global_params, momentum, kept):
    basis = make_basis(kept)
    glob = global_params.astype(jnp.float32)
    local = local_params[0]
    count_rows = glob.shape[0]
    width = glob.shape[1]
    nblocks = width // BLOCK
    replicas = lax.axis_size("replica")
    theirs = local.astype(jnp.float32)
    delta = (glob - theirs).reshape(count_rows, nblocks, BLOCK)
    coef = jnp.einsum("rbn,jn->rbj", delta, basis, precision=lax.Precision.HIGHEST)
    total = lax.psum(
        coef.reshape(count_rows, nblocks * KEEP).astype(jnp.bfloat16), "replica"
    ).astype(jnp.float32)
    new_mom, new_rows = outer_update(total, momentum, glob, basis, replicas)
    params = lax.all_gather(new_rows, "fsdp", axis=0, tiled=True)
    return (params, new_mom)


def solution(mesh):
    in_specs = (P("replica", "fsdp", None), P("fsdp", None), P("fsdp", None), P())
    out_specs = (P(), P("fsdp", None))
    return jax.shard_map(
        on_device, mesh=mesh, in_specs=in_specs, out_specs=out_specs, check_vma=False
    )
```

profile of v0, /device:TPU:1, one launch (start us, length us, event | category | flops | bytes accessed | tf_op | source)
XLA Modules:
  0.0 403.4 jit_solution(15549050359682326967)
XLA Ops:
  7.2 0.0 all-reduce.2.cloned.1.call-start
  7.2 0.7 convert_element_type.35
  7.9 0.7 compare_select_fusion
  8.5 2.7 fusion
  11.3 0.7 copy.18
  12.0 0.0 copy-start.1
  12.0 11.3 %fusion.8 = bf16[128,64,32]{1,2,0:T(8,128)(2,1)S(1)} fusion(f32[128,64,128]{2,1,0:T(8,128)S(1)} %bitcast.17, f32[32]{0:T(128)S(1)} %convert_element_type.35, f32[128]{0:T(128)S(1)} %add_multiply_fusion, f32[32]{0:T(128)S(1)} %compare_select_fusion), kind=kOutput, calls=%fused_computation.13 | convolution fusion | flops 402665472 | bytes 4719360 | tf_op jit(solution)/shard_map/rbn,jn->rbj/dot_general | solution.py:43
  23.3 2.3 copy.17
  25.6 0.0 all-reduce.2.cloned.1.call-update
  25.6 0.2 all-gather.2.cloned.1.call-start
  25.9 0.0 copy-done.1
  25.9 0.3 copy.13
  26.2 150.0 %all-reduce.2.cloned.1.call-done = bf16[128,2048]{0,1:T(8,128)(2,1)} async-done(((bf16[128,2048]{0,1:T(8,128)(2,1)}), bf16[128,2048]{0,1:T(8,128)(2,1)}) %all-reduce.2.cloned.1.call-update) | async-done | bytes 524304 | tf_op jit(solution)/shard_map/psum | solution.py:44
  176.2 1.2 fusion.6
  177.5 5.3 %convolution_multiply_fusion = f32[128,64,128]{0,2,1:T(8,128)} fusion(f32[128,64,32]{0,2,1:T(8,128)S(1)} %bitcast.19, f32[128,64,32]{0,2,1:T(8,128)S(1)} %bitcast.18, f32[32]{0:T(128)S(1)} %convert_element_type.35, f32[128]{0:T(128)S(1)} %add_multiply_fusion, f32[32]{0:T(128)S(1)} %compare_select_fusion), kind=kOutput, calls=%fused_computation.4 | convolution fusion | flops 404500480 | bytes 6292224 | tf_op jit(solution)/shard_map/rbj,jn->rbn/dot_general | solution.py:26
  182.8 0.0 copy-start
  182.8 5.8 %copy.14 = f32[128,8192]{1,0:T(8,128)} copy(f32[128,8192]{0,1:T(8,128)} %bitcast.16) | data formatting | bytes 8388608 | tf_op jit(solution)/shard_map/mul | solution.py:29
  188.6 0.0 copy-done
  188.6 3.9 fusion.1
  192.5 0.0 all-gather.2.cloned.1.call-update
  192.5 1.3 copy.15
  193.8 179.7 %all-gather.2.cloned.1.call-done = bf16[2048,8192]{1,0:T(8,128)(2,1)} async-done(((bf16[128,8192]{1,0:T(8,128)(2,1)}), bf16[2048,8192]{1,0:T(8,128)(2,1)}) %all-gather.2.cloned.1.call-update) | async-done | bytes 33554448 | tf_op jit(solution)/shard_map/all_gather | solution.py:48
  373.5 23.0 %copy.21 = bf16[2048,8192]{1,0:T(8,128)(2,1)} copy(bf16[2048,8192]{1,0:T(8,128)(2,1)} %all-gather.2.cloned.1.call-done) | data formatting | bytes 67108864
  (1 shorter events, 0.0 us)
Async XLA Ops:
  7.2 169.1 %all-reduce.2.cloned.1.call-start = ((), (), s32[]{:S(2)}) async-start(), calls=%async_computation | async-start | bytes 1048576 | tf_op jit(solution)/shard_map/psum | solution.py:44
  12.0 13.9 %copy-start.1 = (f32[128,2048]{1,0:T(8,128)S(1)}, f32[128,2048]{1,0:T(8,128)}, u32[]{:S(2)}) copy-start(f32[128,2048]{1,0:T(8,128)} %param.6) | copy-start | bytes 3145732
  25.6 347.9 %all-gather.2.cloned.1.call-start = ((), (), s32[]{:S(2)}) async-start(), calls=%async_computation.1 | async-start | bytes 35651584 | tf_op jit(solution)/shard_map/all_gather | solution.py:48
  182.8 5.8 %copy-start = (bf16[128,8192]{1,0:T(8,128)(2,1)S(1)}, bf16[128,8192]{1,0:T(8,128)(2,1)}, u32[]{:S(2)}) copy-start(bf16[128,8192]{1,0:T(8,128)(2,1)} %param.5) | copy-start | bytes 6291460
Sparse Core Ops, SparseCore 0:
  25.8 150.4 all-reduce.1
  192.6 180.8 all-gather.1
where the time goes:
time: 404 us; the launch traced here: 403 us
  waiting for transfers between devices  330 us (82%)
  local copies, waits for them, and re-layouts  33.4 us (8%)
  matrix products  16.6 us (4%)
  between operations  14.1 us (3%)
  other arithmetic  9.22 us (2%)
    all_gather x1, waiting for transfers between devices, on_device(): params = lax.all_gather(new_rows, 'fsdp', axis=0, tiled=True)  180 us
    psum x1, waiting for transfers between devices, on_device(): lax.psum(coef.reshape(count_rows, nblocks * KEEP).astype(jnp.bfloat16), '...  150 us
    unnamed x8, local copies, waits for them, and re-layouts  25.4 us
    dot_general x1, matrix products, on_device(): jnp.einsum('rbn,jn->rbj', delta, basis, precision=lax.Precision.HIGHEST)  11.3 us
  transfers between devices with their start and end apart: 2, of which 2 were waited for; matrix products, arithmetic and copies ran while one was open for 0% of the time, Pallas kernels for 0%

commit v1 on v0

v1 whole, which is shorter than its diff:
```python
import jax
import jax.numpy as jnp
from jax import lax
from jax.experimental import pallas as pl
from jax.experimental.pallas import tpu as pltpu
from jax.sharding import PartitionSpec as P

D = 8192
BLOCK = 128
KEEP = 32
ROWS = 2048
SHARD = 128
NZ, NY, NX = 8, 4, 4
REPLICAS = 16
NQ = 4
RQ = SHARD // NQ
GROUPS = 16
GW = D // GROUPS
VMEM = 24 << 20
SPLIT = [(3584, 1536, 384)] * NQ


def here():
    r = lax.axis_index("replica")
    f = lax.axis_index("fsdp")
    x = (r // NZ) * 2 + lax.rem(f // 2, 2)
    return x, f // 4, lax.rem(r, NZ), lax.rem(f, 2)


def device(x, y, z, c):
    x = lax.rem(x + NX, NX)
    y = lax.rem(y + NY, NY)
    z = lax.rem(z + NZ, NZ)
    return ((x // 2) * NZ + z, y * 4 + lax.rem(x, 2) * 2 + c)


def block_mask(shape, row_width, column_width):
    rows = lax.broadcasted_iota(jnp.int32, shape, 0) // row_width
    columns = lax.broadcasted_iota(jnp.int32, shape, 1) // column_width
    return rows == columns


def make_bases(kept_ref, forward, inverse):
    freq = jnp.broadcast_to(kept_ref[...], (BLOCK, 4 * KEEP))
    place = lax.broadcasted_iota(jnp.int32, (BLOCK, 4 * KEEP), 0)
    turn = ((2 * place + 1) * freq) & (4 * BLOCK - 1)
    angle = turn.astype(jnp.float32) * (jnp.pi / (2 * BLOCK))
    scale = jnp.where(freq == 0, (1.0 / BLOCK) ** 0.5, (2.0 / BLOCK) ** 0.5).astype(jnp.float32)
    basis = scale * jnp.cos(angle)
    wide = jnp.concatenate([basis] * 4, axis=0)
    wide = jnp.where(block_mask(wide.shape, BLOCK, KEEP), wide, 0.0)
    high = wide.astype(jnp.bfloat16)
    forward[:, : 4 * KEEP] = high
    forward[:, 4 * KEEP :] = (wide - high.astype(jnp.float32)).astype(jnp.bfloat16)
    back = jnp.concatenate([basis.T * 0.7] * 4, axis=1)
    back = jnp.where(block_mask(back.shape, KEEP, BLOCK), back, 0.0)
    high = back.astype(jnp.bfloat16)
    inverse[: 4 * KEEP, :] = high
    inverse[4 * KEEP :, :] = (back - high.astype(jnp.float32)).astype(jnp.bfloat16)


def outer_kernel(local_ref, glob_ref, mom_in, kept_ref, T, new_mom,
                 lbuf, gbuf, mom, forward, inverse, lhs, coefs, parts, swap_out, swap_in, means,
                 load_sem, send_sem, recv_sem):
    x, y, z, c = here()
    count = [0]
    all_copies = []

    def remote(src, dst, to, landing=None):
        i = count[0]
        count[0] += 1
        copy = pltpu.make_async_remote_copy(
            src, dst, send_sem.at[i], recv_sem.at[i], device_id=to
        )
        copy.start()
        all_copies.append(copy)
        if landing is None:
            return copy
        return pltpu.make_async_remote_copy(
            src, landing, send_sem.at[i], recv_sem.at[i], device_id=to
        )

    def arrive(copies):
        for copy in copies:
            copy.wait_recv()

    sibling = device(x, y, z, 1 - c)
    up, down = device(x, y + 1, z, c), device(x, y - 1, z, c)
    right, left = device(x + 1, y, z, c), device(x - 1, y, z, c)
    far = device(x + 2, y, z, c)
    along = [device(x, y, z + d, c) for d in range(NZ)]
    ahead, behind = along[1], along[NZ - 1]
    barrier = pltpu.get_barrier_semaphore()
    peers = along[1:] + [far, up, down, right, left, sibling]
    for peer in peers:
        pl.semaphore_signal(barrier, inc=1, device_id=peer)

    loads = []
    for q in range(NQ):
        rows = pl.ds(q * RQ, RQ)
        pair = [
            pltpu.make_async_copy(local_ref.at[0, rows], lbuf.at[rows], load_sem.at[2 * q]),
            pltpu.make_async_copy(glob_ref.at[rows], gbuf.at[rows], load_sem.at[2 * q + 1]),
        ]
        for copy in pair:
            copy.start()
        loads.append(pair)
    mom_load = pltpu.make_async_copy(mom_in, mom, load_sem.at[2 * NQ])
    mom_load.start()
    make_bases(kept_ref, forward, inverse)

    st = [dict() for _ in range(NQ)]

    def zi(k):
        return lax.rem(z + k + 2 * NZ, NZ)

    def coefficients(q):
        for copy in loads[q]:
            copy.wait()
        rows = pl.ds(q * RQ, RQ)
        for i in range(GROUPS):
            g = (i % 2) * NZ + i // 2
            cols = pl.ds(g * GW, GW)
            delta = gbuf[rows, cols].astype(jnp.float32) - lbuf[rows, cols].astype(jnp.float32)
            lhs[pl.ds(i * RQ, RQ), :] = delta.astype(jnp.bfloat16)
        both = jnp.dot(lhs[...], forward[...], preferred_element_type=jnp.float32)
        coef = both[:, : 4 * KEEP] + both[:, 4 * KEEP :]
        coefs[q] = coef.astype(jnp.bfloat16).reshape(NZ, 2, RQ, 4 * KEEP)
        if q == 0:
            pl.semaphore_wait(barrier, len(peers))
        st[q]["rs"] = [
            remote(coefs.at[q, zi(d)], parts.at[q, d], along[d]) for d in range(1, NZ)
        ]

    def partial_sum(q):
        arrive(st[q]["rs"])
        total = coefs[q, z].astype(jnp.float32)
        for d in range(1, NZ):
            total = total + parts[q, d].astype(jnp.float32)
        swap_out[q] = total.astype(jnp.bfloat16)
        st[q]["swap"] = [remote(swap_out.at[q], swap_in.at[q], far)]

    def mean(q):
        arrive(st[q]["swap"])
        total = swap_out[q].astype(jnp.float32) + swap_in[q].astype(jnp.float32)
        means[q, z] = (total * (1.0 / REPLICAS)).astype(jnp.bfloat16)
        st[q]["mean"] = [
            remote(means.at[q, z], means.at[q, z], along[d], means.at[q, zi(-d)])
            for d in range(1, NZ)
        ]

    def new_rows(q):
        arrive(st[q]["mean"])
        if q == 0:
            mom_load.wait()
        rows = pl.ds(q * RQ, RQ)
        steps = []
        for i in range(GROUPS):
            g = (i % 2) * NZ + i // 2
            cols = pl.ds(g * 4 * KEEP, 4 * KEEP)
            avg = means[q, i // 2, i % 2].astype(jnp.float32)
            fresh = 0.9 * mom[rows, cols] + avg
            new_mom[rows, cols] = fresh
            step = (avg + 0.9 * fresh).astype(jnp.bfloat16)
            lhs[pl.ds(i * RQ, RQ), : 4 * KEEP] = step
            lhs[pl.ds(i * RQ, RQ), 4 * KEEP : 8 * KEEP] = step
        update = jnp.dot(lhs[:, : 8 * KEEP], inverse[...], preferred_element_type=jnp.float32)
        for i in range(GROUPS):
            g = (i % 2) * NZ + i // 2
            cols = pl.ds(g * GW, GW)
            mine = gbuf[rows, cols].astype(jnp.float32) - update[i * RQ : (i + 1) * RQ]
            T[0, 0, 0, rows, cols] = mine.astype(jnp.bfloat16)

    def geometry(q):
        a1, a2, b = SPLIT[q]
        a = a1 + a2
        rows = pl.ds(q * RQ, RQ)
        first, second = pl.ds(q * RQ, RQ // 2), pl.ds(q * RQ + RQ // 2, RQ // 2)
        def strip(k):
            return pl.ds(pl.multiple_of(a + zi(k) * b, 128), b)
        return a1, a2, a, b, rows, first, second, strip

    def g0(q):
        a1, a2, a, b, rows, first, second, strip = geometry(q)
        every, h0, h1, s = pl.ds(0, a), pl.ds(0, a // 2), pl.ds(a // 2, a // 2), strip(0)
        s_ = st[q]
        s_["y1"] = [
            remote(T.at[0, 0, 0, rows, every], T.at[0, 3, 0, rows, every], up),
            remote(T.at[0, 0, 0, rows, every], T.at[0, 1, 0, rows, every], down),
        ]
        s_["x1"] = [
            remote(T.at[0, 0, 0, rows, h0], T.at[0, 0, 1, rows, h0], right),
            remote(T.at[0, 0, 0, rows, h1], T.at[0, 0, 1, rows, h1], left),
        ]
        if b:
            s_["y1"] += [
                remote(T.at[0, 0, 0, rows, s], T.at[0, 3, 0, rows, s], up),
                remote(T.at[0, 0, 0, rows, s], T.at[0, 1, 0, rows, s], down),
            ]
            s_["bx1"] = [
                remote(T.at[0, 0, 0, first, s], T.at[0, 0, 1, first, s], right),
                remote(T.at[0, 0, 0, second, s], T.at[0, 0, 1, second, s], left),
            ]
        s_["d2d"] = [remote(T.at[0, 0, 0, rows], T.at[1, 0, 0, rows], sibling)]

    def g1(q):
        a1, a2, a, b, rows, first, second, strip = geometry(q)
        h0, h1, s = pl.ds(0, a // 2), pl.ds(a // 2, a // 2), strip(0)
        mid = pl.ds(a1 // 2, a2)
        s_ = st[q]
        arrive(s_["y1"])
        s_["y2"] = [
            remote(T.at[0, 3, 0, rows, h0], T.at[0, 2, 0, rows, h0], up),
            remote(T.at[0, 1, 0, rows, h1], T.at[0, 2, 0, rows, h1], down),
        ]
        if b:
            s_["y2"] += [
                remote(T.at[0, 3, 0, first, s], T.at[0, 2, 0, first, s], up),
                remote(T.at[0, 1, 0, second, s], T.at[0, 2, 0, second, s], down),
            ]
        arrive(s_["x1"])
        s_["xy1"] = []
        if a2:
            s_["xy1"] = [
                remote(T.at[0, 0, 1, rows, mid], T.at[0, 3, 1, rows, mid], up),
                remote(T.at[0, 0, 1, rows, mid], T.at[0, 1, 1, rows, mid], down),
            ]

    def g2(q):
        a1, a2, a, b, rows, first, second, strip = geometry(q)
        s = strip(0)
        o0, o1 = pl.ds(0, a1 // 2), pl.ds(a1 // 2 + a2, a1 // 2)
        m0, m1 = pl.ds(a1 // 2, a2 // 2), pl.ds(a1 // 2 + a2 // 2, a2 // 2)
        three = pl.ds(1, 3)
        s_ = st[q]
        arrive(s_["y2"])
        s_["x2"] = [
            remote(T.at[0, three, 0, rows, o0], T.at[0, three, 1, rows, o0], right),
            remote(T.at[0, three, 0, rows, o1], T.at[0, three, 1, rows, o1], left),
        ]
        if b:
            s_["bx2"] = [
                remote(T.at[0, three, 0, first, s], T.at[0, three, 1, first, s], right),
                remote(T.at[0, three, 0, second, s], T.at[0, three, 1, second, s], left),
            ]
        arrive(s_["xy1"])
        s_["xy2"] = []
        if a2:
            s_["xy2"] = [
                remote(T.at[0, 3, 1, rows, m0], T.at[0, 2, 1, rows, m0], up),
                remote(T.at[0, 1, 1, rows, m1], T.at[0, 2, 1, rows, m1], down),
            ]
        every = pl.ds(0, a)
        s_["d2d"] += [
            remote(T.at[0, three, 0, rows, every], T.at[1, three, 0, rows, every], sibling)
        ]

    pieces = [(0, 1), (pl.ds(1, 3), slice(None))]

    def z_hop(q, hop):
        a1, a2, a, b, rows, first, second, strip = geometry(q)
        out = []
        for dy, dx in pieces:
            for to, sign in ((ahead, -1), (behind, 1)):
                r = rows if hop < 3 else (first if sign < 0 else second)
                s = strip(sign * hop)
                land = strip(sign * (hop + 1))
                out.append(remote(T.at[0, dy, dx, r, s], T.at[0, dy, dx, r, s], to,
                                  T.at[0, dy, dx, r, land]))
        st[q]["z%d" % hop] = out

    def g3(q):
        a1, a2, a, b, rows, first, second, strip = geometry(q)
        s_ = st[q]
        if b:
            arrive(s_["bx1"] + s_["bx2"])
            z_hop(q, 0)
        arrive(s_["x2"] + s_["xy2"])
        every = pl.ds(0, a)
        s_["d2d"] += [remote(T.at[0, :, 1, rows, every], T.at[1, :, 1, rows, every], sibling)]

    def later_hop(hop):
        def go(q):
            if SPLIT[q][2]:
                arrive(st[q]["z%d" % (hop - 1)])
                z_hop(q, hop)
        return go

    def g7(q):
        a1, a2, a, b, rows, first, second, strip = geometry(q)
        if b:
            arrive(st[q]["z3"])
            rest = pl.ds(a, D - a)
            st[q]["d2d"] += [
                remote(T.at[0, dy, dx, rows, rest], T.at[1, dy, dx, rows, rest], sibling)
                for dy, dx in pieces
            ]

    def finish(q):
        arrive(st[q]["d2d"])

    first_part = [coefficients, partial_sum, mean]
    second_part = [lambda q: (new_rows(q), g0(q)), g1, g2, g3] + [later_hop(h) for h in (1, 2, 3)] + [g7]
    stages = first_part + second_part
    for wave in range(len(stages) + NQ - 1):
        for q in reversed(range(NQ)):
            k = wave - q
            if 0 <= k < len(stages):
                stages[k](q)
    for q in range(NQ):
        finish(q)
    for copy in all_copies:
        copy.wait_send()


NSEM = 64 * NQ


def place_kernel(T, mom, params, new_mom, sem):
    x, y, z, c = here()
    copies = [pltpu.make_async_copy(mom, new_mom, sem.at[16])]
    for p in range(2):
        for dy in range(4):
            for dx in range(2):
                shard = (
                    lax.rem(y + dy, NY) * 4 + lax.rem(x + dx, 2) * 2 + lax.rem(c + p, 2)
                )
                rows = pl.ds(pl.multiple_of(shard * SHARD, SHARD), SHARD)
                copies.append(
                    pltpu.make_async_copy(
                        T.at[p, dy, dx], params.at[rows], sem.at[(p * 4 + dy) * 2 + dx]
                    )
                )
    for copy in copies:
        copy.start()
    for copy in copies:
        copy.wait()


def on_device(local_params, global_params, momentum, kept):
    lanes = jnp.tile(kept, 4)[None, :]
    bf16, f32 = jnp.bfloat16, jnp.float32
    anywhere = pl.BlockSpec(memory_space=pl.ANY)
    in_vmem = pl.BlockSpec(memory_space=pltpu.VMEM)
    T, mom = pl.pallas_call(
        outer_kernel,
        out_shape=(pltpu.VMEM((2, 4, 2, SHARD, D), bf16), pltpu.VMEM((SHARD, D // 4), f32)),
        in_specs=[anywhere, anywhere, anywhere, in_vmem],
        out_specs=(in_vmem, in_vmem),
        scratch_shapes=[
            pltpu.VMEM((SHARD, D), bf16),
            pltpu.VMEM((SHARD, D), bf16),
            pltpu.VMEM((SHARD, D // 4), f32),
            pltpu.VMEM((GW, 8 * KEEP), bf16),
            pltpu.VMEM((8 * KEEP, GW), bf16),
            pltpu.VMEM((GROUPS * RQ, GW), bf16),
            pltpu.VMEM((NQ, NZ, 2, RQ, 4 * KEEP), bf16),
            pltpu.VMEM((NQ, NZ, 2, RQ, 4 * KEEP), bf16),
            pltpu.VMEM((NQ, 2, RQ, 4 * KEEP), bf16),
            pltpu.VMEM((NQ, 2, RQ, 4 * KEEP), bf16),
            pltpu.VMEM((NQ, NZ, 2, RQ, 4 * KEEP), bf16),
            pltpu.SemaphoreType.DMA((2 * NQ + 1,)),
            pltpu.SemaphoreType.DMA((NSEM,)),
            pltpu.SemaphoreType.DMA((NSEM,)),
        ],
        compiler_params=pltpu.CompilerParams(
            collective_id=0, has_side_effects=True, vmem_limit_bytes=VMEM
        ),
    )(local_params, global_params, momentum, lanes)
    return pl.pallas_call(
        place_kernel,
        out_shape=(
            jax.ShapeDtypeStruct((ROWS, D), bf16),
            jax.ShapeDtypeStruct((SHARD, D // 4), f32),
        ),
        in_specs=[in_vmem, in_vmem],
        out_specs=(anywhere, anywhere),
        scratch_shapes=[pltpu.SemaphoreType.DMA((17,))],
        compiler_params=pltpu.CompilerParams(vmem_limit_bytes=VMEM),
    )(
        pltpu.with_memory_space_constraint(T, pltpu.VMEM),
        pltpu.with_memory_space_constraint(mom, pltpu.VMEM),
    )


def solution(mesh):
    in_specs = (P("replica", "fsdp", None), P("fsdp", None), P("fsdp", None), P())
    out_specs = (P(), P("fsdp", None))
    return jax.shard_map(
        on_device, mesh=mesh, in_specs=in_specs, out_specs=out_specs, check_vma=False
    )
```

time: 404 us -> 150 us (0.37)
  waiting for transfers between devices: 330 us -> 0 us
  Pallas kernels: 0 us -> 148 us
  local copies, waits for them, and re-layouts: 33.4 us -> 1.25 us
  matrix products: 16.6 us -> 0 us
  between operations: 14.1 us -> 0.64 us
  other arithmetic: 9.22 us -> 0 us
    all_gather x1 -> x0, waiting for transfers between devices: 180 us -> none  [on_device(): params = lax.all_gather(new_rows, 'fsdp', axis=0, tiled=True)]
    psum x1 -> x0, waiting for transfers between devices: 150 us -> none  [on_device(): lax.psum(coef.reshape(count_rows, nblocks * KEEP).astype(jnp.bfloat16), '...]
    pallas_call x0 -> x2, Pallas kernels: none -> 148 us  [the longest x1 136 us: on_device(): pl.pallas_call(outer_kernel, out_shape=(pltpu.VMEM((2, 4, 2, SHARD, D), b...]
    unnamed x8 -> x0, local copies, waits for them, and re-layouts: 25.4 us -> none
    dot_general x2 -> x0, matrix products: 16.6 us -> none  [the longest x1 11.3 us: on_device(): jnp.einsum('rbn,jn->rbj', delta, basis, precision=lax.Precision.HIGHEST)]
    mul x1 -> x0, local copies, waits for them, and re-layouts: 5.77 us -> none  [outer_update(): new_rows = (glob - 0.7 * update).astype(jnp.bfloat16)]
    convert_element_type x2 -> x0, other arithmetic: 4.58 us -> none  [the longest x1 3.92 us: outer_update(): new_rows = (glob - 0.7 * update).astype(jnp.bfloat16)]
  transfers between devices with their start and end apart: 2 -> 0, of which waited for: 2 -> 0; matrix products, arithmetic and copies ran while one was open for 0% -> 0% of each run, Pallas kernels for 0% -> 0%
where the time goes in v1:
time: 150 us; the launch traced here: 149 us
  Pallas kernels  148 us (99%)
    pallas_call x1, Pallas kernels, on_device(): pl.pallas_call(outer_kernel, out_shape=(pltpu.VMEM((2, 4, 2, SHARD, D), b...  136 us
    pallas_call x1, Pallas kernels, on_device(): pl.pallas_call(place_kernel, out_shape=(jax.ShapeDtypeStruct((ROWS, D), b...  11.4 us

profile of v1, /device:TPU:1, one launch (start us, length us, event | category | flops | bytes accessed | tf_op | source)
XLA Modules:
  0.0 149.5 jit_solution(3383736104967052846)
XLA Ops:
  0.6 0.7 tile.2
  1.3 0.6 broadcast_in_dim_tile.3.kept_ref
  1.9 136.2 %shard_map.59 = (bf16[2,4,2,128,8192]{4,3,2,1,0:T(8,128)(2,1)S(1)}, f32[128,2048]{1,0:T(8,128)S(1)}) custom-call(bf16[1,128,8192]{2,1,0:T(8,128)(2,1)} %local_ref.1, bf16[128,8192]{1,0:T(8,128)(2,1)} %glob_ref.1, f32[128,2048]{1,0:T(8,128)} %mom_in.1, s32[1,128]{1,0:T(1,128)} %broadcast_in_dim_tile.3.kept_ref), custom_call_target="tpu_custom_call" | custom-call | tf_op jit(solution)/shard_map/pallas_call | solution.py:345
  138.1 11.4 %shard_map.60 = (bf16[2048,8192]{1,0:T(8,128)(2,1)}, f32[128,2048]{1,0:T(8,128)}) custom-call(bf16[2,4,2,128,8192]{4,3,2,1,0:T(8,128)(2,1)S(1)} %get-tuple-element.4.T, f32[128,2048]{1,0:T(8,128)S(1)} %get-tuple-element.5.mom), custom_call_target="tpu_custom_call" | custom-call | tf_op jit(solution)/shard_map/pallas_call | solution.py:370

commit v2 on v1

v2 whole, which is shorter than its diff:
```python
import jax
import jax.numpy as jnp
from jax import lax
from jax.experimental import pallas as pl
from jax.experimental.pallas import tpu as pltpu
from jax.sharding import PartitionSpec as P

D = 8192
BLOCK = 128
KEEP = 32
ROWS = 2048
SHARD = 128
NZ, NY, NX = 8, 4, 4
REPLICAS = 16
GROUPS = 16
GW = D // GROUPS
VMEM = 24 << 20
CHUNKS = [(0, 32), (32, 32), (64, 32), (96, 32)]
NQ = len(CHUNKS)
SPLIT = [(3072, 0, 640), (5120, 0, 384), (4608, 2560, 128), (4864, 2304, 128)]
SEMAPHORES = 190
ORDER = [
    ("coef", 0), ("coef", 1), ("coef", 2), ("sum", 0), ("coef", 3), ("sum", 1), ("mean", 0), ("sum", 2),
    ("mean", 1), ("sum", 3), ("mean", 2), ("rows", 0), ("oyB", 0), ("ox1", 0), ("oxB", 0), ("oy", 0), ("od", 0),
    ("rows", 1), ("yB2", 0), ("oyB", 1), ("ox1", 1), ("oxB", 1), ("oy", 1), ("od", 1), ("mean", 3), ("rows", 2),
    ("xB2", 0), ("x2a", 0), ("yB2", 1), ("oxB", 2), ("oy", 2), ("od", 2), ("rows", 3), ("z0", 0), ("oxB", 3),
    ("oy", 3), ("od", 3), ("ox2", 2), ("xB2", 1), ("x2a", 1), ("ay1", 2), ("z0", 1), ("z1", 0), ("x2a", 2),
    ("z1", 1), ("oyB", 2), ("oyB", 3), ("x2a", 3), ("y2", 0), ("z2", 0), ("y2", 1), ("yB2", 2), ("yB2", 3),
    ("x2b", 0), ("d1", 0), ("z2", 1), ("ay0", 2), ("xB2", 3), ("x2b", 1), ("d1", 1), ("xB2", 2), ("y2", 2),
    ("z3", 0), ("d2", 0), ("ay2", 2), ("ox1", 2), ("z3", 1), ("x2b", 2), ("d1", 2), ("ay0", 3), ("d2", 1),
    ("z0", 2), ("z0", 3), ("d3", 2), ("y2", 3), ("ox2", 3), ("d4", 1), ("ox1", 3), ("d4", 0), ("d2", 2),
    ("z1", 2), ("z1", 3), ("ay1", 3), ("x2b", 3), ("d1", 3), ("z2", 2), ("z2", 3), ("z3", 2), ("ay2", 3),
    ("z3", 3), ("d2", 3), ("d4", 2), ("d4", 3), ("d3", 3),
]


def here():
    r = lax.axis_index("replica")
    f = lax.axis_index("fsdp")
    x = (r // NZ) * 2 + lax.rem(f // 2, 2)
    return x, f // 4, lax.rem(r, NZ), lax.rem(f, 2)


def device(x, y, z, c):
    x = lax.rem(x + NX, NX)
    y = lax.rem(y + NY, NY)
    z = lax.rem(z + NZ, NZ)
    return ((x // 2) * NZ + z, y * 4 + lax.rem(x, 2) * 2 + c)


def block_mask(shape, row_width, column_width):
    rows = lax.broadcasted_iota(jnp.int32, shape, 0) // row_width
    columns = lax.broadcasted_iota(jnp.int32, shape, 1) // column_width
    return rows == columns


def make_bases(kept_ref, forward, inverse):
    lanes = jnp.concatenate([kept_ref[...]] * 4, axis=1)
    freq = jnp.broadcast_to(lanes, (BLOCK, 4 * KEEP))
    place = lax.broadcasted_iota(jnp.int32, (BLOCK, 4 * KEEP), 0)
    turn = ((2 * place + 1) * freq) & (4 * BLOCK - 1)
    angle = turn.astype(jnp.float32) * (jnp.pi / (2 * BLOCK))
    scale = jnp.where(freq == 0, (1.0 / BLOCK) ** 0.5, (2.0 / BLOCK) ** 0.5).astype(jnp.float32)
    basis = scale * jnp.cos(angle)
    wide = jnp.concatenate([basis] * 4, axis=0)
    wide = jnp.where(block_mask(wide.shape, BLOCK, KEEP), wide, 0.0)
    high = wide.astype(jnp.bfloat16)
    forward[:, : 4 * KEEP] = high
    forward[:, 4 * KEEP :] = (wide - high.astype(jnp.float32)).astype(jnp.bfloat16)
    back = jnp.concatenate([basis.T * 0.7] * 4, axis=1)
    back = jnp.where(block_mask(back.shape, KEEP, BLOCK), back, 0.0)
    high = back.astype(jnp.bfloat16)
    inverse[: 4 * KEEP, :] = high
    inverse[4 * KEEP :, :] = (back - high.astype(jnp.float32)).astype(jnp.bfloat16)


def outer_kernel(local_ref, glob_ref, mom_in, kept_ref, T, new_mom,
                 lbuf, gbuf, mom, forward, inverse, lhs, coefs, parts, swap_out, swap_in, means,
                 load_sem, send_sem, recv_sem):
    x, y, z, c = here()
    all_copies = []

    def remote(src, dst, to, landing=None):
        i = len(all_copies)
        copy = pltpu.make_async_remote_copy(
            src, dst, send_sem.at[i], recv_sem.at[i], device_id=to
        )
        copy.start()
        all_copies.append(copy)
        if landing is None:
            return copy
        return pltpu.make_async_remote_copy(
            src, landing, send_sem.at[i], recv_sem.at[i], device_id=to
        )

    flying = {}

    def arrive(*names):
        for name in names:
            for copy in flying.pop(name, []):
                copy.wait_recv()

    sibling = device(x, y, z, 1 - c)
    up, down = device(x, y + 1, z, c), device(x, y - 1, z, c)
    right, left = device(x + 1, y, z, c), device(x - 1, y, z, c)
    far = device(x + 2, y, z, c)
    along = [device(x, y, z + d, c) for d in range(NZ)]
    ahead, behind = along[1], along[NZ - 1]
    barrier = pltpu.get_barrier_semaphore()
    peers = along[1:] + [far, up, down, right, left, sibling]
    for peer in peers:
        pl.semaphore_signal(barrier, inc=1, device_id=peer)

    loads = []
    for q, (start, size) in enumerate(CHUNKS):
        rows = pl.ds(start, size)
        pair = [
            pltpu.make_async_copy(local_ref.at[0, rows], lbuf.at[rows], load_sem.at[2 * q]),
            pltpu.make_async_copy(glob_ref.at[rows], gbuf.at[rows], load_sem.at[2 * q + 1]),
        ]
        for copy in pair:
            copy.start()
        loads.append(pair)
    mom_load = pltpu.make_async_copy(mom_in, mom, load_sem.at[2 * NQ])
    mom_load.start()
    make_bases(kept_ref, forward, inverse)

    def zi(k):
        return lax.rem(z + k + 2 * NZ, NZ)

    def column_group(i):
        return (i % 2) * NZ + i // 2

    def coef(q):
        for copy in loads[q]:
            copy.wait()
        start, size = CHUNKS[q]
        rows = pl.ds(start, size)
        for i in range(GROUPS):
            cols = pl.ds(column_group(i) * GW, GW)
            delta = gbuf[rows, cols].astype(jnp.float32) - lbuf[rows, cols].astype(jnp.float32)
            lhs[pl.ds(i * size, size), :] = delta.astype(jnp.bfloat16)
        both = jnp.dot(
            lhs[: GROUPS * size], forward[...], preferred_element_type=jnp.float32
        )
        out = both[:, : 4 * KEEP] + both[:, 4 * KEEP :]
        coefs[:, :, rows] = out.astype(jnp.bfloat16).reshape(NZ, 2, size, 4 * KEEP)
        if q == 0:
            pl.semaphore_wait(barrier, len(peers))
        return [
            remote(coefs.at[zi(d), :, rows], parts.at[d, :, rows], along[d])
            for d in range(1, NZ)
        ]

    def partial_sum(q):
        arrive(("coef", q))
        rows = pl.ds(*CHUNKS[q])
        total = coefs[z, :, rows].astype(jnp.float32)
        for d in range(1, NZ):
            total = total + parts[d, :, rows].astype(jnp.float32)
        swap_out[:, rows] = total.astype(jnp.bfloat16)
        return [remote(swap_out.at[:, rows], swap_in.at[:, rows], far)]

    def mean(q):
        arrive(("sum", q))
        rows = pl.ds(*CHUNKS[q])
        total = swap_out[:, rows].astype(jnp.float32) + swap_in[:, rows].astype(jnp.float32)
        means[z, :, rows] = (total * (1.0 / REPLICAS)).astype(jnp.bfloat16)
        return [
            remote(means.at[z, :, rows], means.at[z, :, rows], along[d],
                   means.at[zi(-d), :, rows])
            for d in range(1, NZ)
        ]

    def new_rows(q):
        arrive(("mean", q))
        if q == 0:
            mom_load.wait()
        start, size = CHUNKS[q]
        rows = pl.ds(start, size)
        for i in range(GROUPS):
            cols = pl.ds(column_group(i) * 4 * KEEP, 4 * KEEP)
            avg = means[i // 2, i % 2, rows].astype(jnp.float32)
            fresh = 0.9 * mom[rows, cols] + avg
            new_mom[rows, cols] = fresh
            step = (avg + 0.9 * fresh).astype(jnp.bfloat16)
            lhs[pl.ds(i * size, size), : 4 * KEEP] = step
            lhs[pl.ds(i * size, size), 4 * KEEP : 8 * KEEP] = step
        update = jnp.dot(
            lhs[: GROUPS * size, : 8 * KEEP], inverse[...], preferred_element_type=jnp.float32
        )
        for i in range(GROUPS):
            cols = pl.ds(column_group(i) * GW, GW)
            mine = gbuf[rows, cols].astype(jnp.float32) - update[i * size : (i + 1) * size]
            T[0, 0, rows, cols] = mine.astype(jnp.bfloat16)
        return []

    def pass_on(q, name):
        a1, a2, b = SPLIT[q]
        a = a1 + a2
        rows = pl.ds(*CHUNKS[q])
        odd = q % 2
        p, p0, p1 = pl.ds(0, a1), pl.ds(0, a1 // 2), pl.ds(a1 // 2, a1 // 2)
        s, s0, s1 = pl.ds(a1, a2), pl.ds(a1, a2 // 2), pl.ds(a1 + a2 // 2, a2 // 2)

        def strip(k):
            return pl.ds(pl.multiple_of(a + zi(k) * b, 128), b)

        def send(slot, to_slot, cols, to, landing=None):
            return remote(
                T.at[0, slot, rows, cols], T.at[0, to_slot, rows, cols], to,
                None if landing is None else T.at[0, to_slot, rows, landing],
            )

        def share(slot, cols):
            return [remote(T.at[0, slot, rows, cols], T.at[1, slot, rows, cols], sibling)]

        near, away = pl.ds(1, 3), pl.ds(5, 3)
        others = pl.ds(1, 7)
        if name == "ox1":
            return [send(0, 4, p0, right), send(0, 4, p1, left)]
        if name == "oy":
            return [send(0, 3, p, up), send(0, 1, p, down)]
        if name == "od":
            return share(0, pl.ds(0, D))
        if name == "y2":
            arrive(("oy", q))
            return [send(3, 2, p0, up), send(1, 2, p1, down)]
        if name == "x2a":
            arrive(("oy", q))
            return [send(i, i + 4, h, to) for i in (1, 3) for h, to in ((p0, right), (p1, left))]
        if name == "x2b":
            arrive(("y2", q))
            return [send(2, 6, p0, right), send(2, 6, p1, left)]
        if name == "d1":
            arrive(("oy", q), ("y2", q))
            return share(near, p)
        if name == "d2":
            arrive(("ox1", q), ("x2a", q), ("x2b", q))
            return share(pl.ds(4, 4), p)
        if name == "ox2":
            return [send(0, 4, s0, right), send(0, 4, s1, left)]
        if name == "ay0":
            return [send(0, 3, s, up), send(0, 1, s, down)]
        if name == "ay1":
            arrive(("ox2", q))
            return [send(4, 7, s, up), send(4, 5, s, down)]
        if name == "ay2":
            arrive(("ay0", q), ("ay1", q))
            return [send(3, 2, s, up), send(5, 6, s, down)]
        if name == "d3":
            arrive(("ay2", q))
            return share(others, s)
        mine = strip(0)
        if name == "oyB":
            return [send(0, 3, mine, up), send(0, 1, mine, down)]
        if name == "oxB":
            return [send(0, 4, mine, right if odd else left)]
        if name == "yB2":
            arrive(("oyB", q))
            return [send(1, 2, mine, down) if odd else send(3, 2, mine, up)]
        if name == "xB2":
            arrive(("yB2", q))
            return [send(near, away, mine, left if odd else right)]
        if name == "d4":
            arrive(("z3", q))
            return share(others, pl.ds(a, D - a))
        hop = int(name[1])
        arrive(*((("xB2", q), ("oxB", q)) if hop == 0 else (("z%d" % (hop - 1), q),)))
        onward = [
            (strip(-hop), ahead, strip(-hop - 1)),
            (strip(hop), behind, strip(hop + 1)),
        ]
        if hop == 3:
            onward = onward[odd : odd + 1]
        return [send(others, others, cols, to, landing) for cols, to, landing in onward]

    compute = {"coef": coef, "sum": partial_sum, "mean": mean, "rows": new_rows}
    for name, q in ORDER:
        if name in compute:
            flying[name, q] = compute[name](q)
        else:
            flying[name, q] = pass_on(q, name)
    arrive(*list(flying))
    for copy in all_copies:
        copy.wait_send()


def place_kernel(T, mom, params, new_mom, sem):
    x, y, z, c = here()
    copies = [pltpu.make_async_copy(mom, new_mom, sem.at[16])]
    for p in range(2):
        for dy in range(4):
            for dx in range(2):
                slot = dx * 4 + dy
                shard = (
                    lax.rem(y + dy, NY) * 4 + lax.rem(x + dx, 2) * 2 + lax.rem(c + p, 2)
                )
                rows = pl.ds(pl.multiple_of(shard * SHARD, SHARD), SHARD)
                copies.append(
                    pltpu.make_async_copy(
                        T.at[p, slot], params.at[rows], sem.at[p * 8 + slot]
                    )
                )
    for copy in copies:
        copy.start()
    for copy in copies:
        copy.wait()


def on_device(local_params, global_params, momentum, kept):
    lanes = kept[None, :]
    bf16, f32 = jnp.bfloat16, jnp.float32
    anywhere = pl.BlockSpec(memory_space=pl.ANY)
    in_vmem = pl.BlockSpec(memory_space=pltpu.VMEM)
    T, mom = pl.pallas_call(
        outer_kernel,
        out_shape=(pltpu.VMEM((2, 8, SHARD, D), bf16), pltpu.VMEM((SHARD, D // 4), f32)),
        in_specs=[anywhere, anywhere, anywhere, in_vmem],
        out_specs=(in_vmem, in_vmem),
        scratch_shapes=[
            pltpu.VMEM((SHARD, D), bf16),
            pltpu.VMEM((SHARD, D), bf16),
            pltpu.VMEM((SHARD, D // 4), f32),
            pltpu.VMEM((GW, 8 * KEEP), bf16),
            pltpu.VMEM((8 * KEEP, GW), bf16),
            pltpu.VMEM((GROUPS * max(size for _, size in CHUNKS), GW), bf16),
            pltpu.VMEM((NZ, 2, SHARD, 4 * KEEP), bf16),
            pltpu.VMEM((NZ, 2, SHARD, 4 * KEEP), bf16),
            pltpu.VMEM((2, SHARD, 4 * KEEP), bf16),
            pltpu.VMEM((2, SHARD, 4 * KEEP), bf16),
            pltpu.VMEM((NZ, 2, SHARD, 4 * KEEP), bf16),
            pltpu.SemaphoreType.DMA((2 * NQ + 1,)),
            pltpu.SemaphoreType.DMA((SEMAPHORES,)),
            pltpu.SemaphoreType.DMA((SEMAPHORES,)),
        ],
        compiler_params=pltpu.CompilerParams(
            collective_id=0, has_side_effects=True, vmem_limit_bytes=VMEM
        ),
    )(local_params, global_params, momentum, lanes)
    return pl.pallas_call(
        place_kernel,
        out_shape=(
            jax.ShapeDtypeStruct((ROWS, D), bf16),
            jax.ShapeDtypeStruct((SHARD, D // 4), f32),
        ),
        in_specs=[in_vmem, in_vmem],
        out_specs=(anywhere, anywhere),
        scratch_shapes=[pltpu.SemaphoreType.DMA((17,))],
        compiler_params=pltpu.CompilerParams(vmem_limit_bytes=VMEM),
    )(
        pltpu.with_memory_space_constraint(T, pltpu.VMEM),
        pltpu.with_memory_space_constraint(mom, pltpu.VMEM),
    )


def solution(mesh):
    in_specs = (P("replica", "fsdp", None), P("fsdp", None), P("fsdp", None), P())
    out_specs = (P(), P("fsdp", None))
    return jax.shard_map(
        on_device, mesh=mesh, in_specs=in_specs, out_specs=out_specs, check_vma=False
    )
```

time: 150 us -> 113 us (0.75)
  Pallas kernels: 148 us -> 112 us
    pallas_call x1, Pallas kernels: 136 us -> 101 us  [on_device(): pl.pallas_call(outer_kernel, out_shape=(pltpu.VMEM((2, 8, SHARD, D), bf16...]
where the time goes in v2:
time: 113 us
  Pallas kernels  112 us (99%)
    pallas_call x1, Pallas kernels, on_device(): pl.pallas_call(outer_kernel, out_shape=(pltpu.VMEM((2, 8, SHARD, D), bf16...  101 us
    pallas_call x1, Pallas kernels, on_device(): pl.pallas_call(place_kernel, out_shape=(jax.ShapeDtypeStruct((ROWS, D), b...  11.4 us

profile of v2, /device:TPU:1, one launch (start us, length us, event | category | flops | bytes accessed | tf_op | source)
XLA Modules:
  0.0 112.7 jit_solution(3318105897089989299)
XLA Ops:
  0.6 100.6 %shard_map.59 = (bf16[2,8,128,8192]{3,2,1,0:T(8,128)(2,1)S(1)}, f32[128,2048]{1,0:T(8,128)S(1)}) custom-call(bf16[1,128,8192]{2,1,0:T(8,128)(2,1)} %local_ref.1, bf16[128,8192]{1,0:T(8,128)(2,1)} %glob_ref.1, f32[128,2048]{1,0:T(8,128)} %mom_in.1, s32[1,32]{1,0:T(1,128)} %bitcast.1), custom_call_target="tpu_custom_call" | custom-call | tf_op jit(solution)/shard_map/pallas_call | solution.py:316
  101.3 11.4 %shard_map.60 = (bf16[2048,8192]{1,0:T(8,128)(2,1)}, f32[128,2048]{1,0:T(8,128)}) custom-call(bf16[2,8,128,8192]{3,2,1,0:T(8,128)(2,1)S(1)} %get-tuple-element.4.T, f32[128,2048]{1,0:T(8,128)S(1)} %get-tuple-element.5.mom), custom_call_target="tpu_custom_call" | custom-call | tf_op jit(solution)/shard_map/pallas_call | solution.py:341

commit v3 on v2

--- a/solution.py
+++ b/solution.py
@@ -15,22 +15,26 @@
 GROUPS = 16
 GW = D // GROUPS
 VMEM = 24 << 20
-CHUNKS = [(0, 32), (32, 32), (64, 32), (96, 32)]
+CHUNKS = [(0, 48), (48, 16), (64, 32), (96, 32)]
 NQ = len(CHUNKS)
-SPLIT = [(3072, 0, 640), (5120, 0, 384), (4608, 2560, 128), (4864, 2304, 128)]
-SEMAPHORES = 190
+SPLIT = {0: (2048, 0, 0), 1: (5120, 0, 384), 2: (4608, 1536, 256), 3: (3840, 1280, 384), 'raw': (2560, 3584, 256)}
+SHARES = ("od", "d1", "d2", "d3", "d4")
+SEMAPHORES = 214
 ORDER = [
-    ("coef", 0), ("coef", 1), ("coef", 2), ("sum", 0), ("coef", 3), ("sum", 1), ("mean", 0), ("sum", 2),
-    ("mean", 1), ("sum", 3), ("mean", 2), ("rows", 0), ("oyB", 0), ("ox1", 0), ("oxB", 0), ("oy", 0), ("od", 0),
-    ("rows", 1), ("yB2", 0), ("oyB", 1), ("ox1", 1), ("oxB", 1), ("oy", 1), ("od", 1), ("mean", 3), ("rows", 2),
-    ("xB2", 0), ("x2a", 0), ("yB2", 1), ("oxB", 2), ("oy", 2), ("od", 2), ("rows", 3), ("z0", 0), ("oxB", 3),
-    ("oy", 3), ("od", 3), ("ox2", 2), ("xB2", 1), ("x2a", 1), ("ay1", 2), ("z0", 1), ("z1", 0), ("x2a", 2),
-    ("z1", 1), ("oyB", 2), ("oyB", 3), ("x2a", 3), ("y2", 0), ("z2", 0), ("y2", 1), ("yB2", 2), ("yB2", 3),
-    ("x2b", 0), ("d1", 0), ("z2", 1), ("ay0", 2), ("xB2", 3), ("x2b", 1), ("d1", 1), ("xB2", 2), ("y2", 2),
-    ("z3", 0), ("d2", 0), ("ay2", 2), ("ox1", 2), ("z3", 1), ("x2b", 2), ("d1", 2), ("ay0", 3), ("d2", 1),
-    ("z0", 2), ("z0", 3), ("d3", 2), ("y2", 3), ("ox2", 3), ("d4", 1), ("ox1", 3), ("d4", 0), ("d2", 2),
-    ("z1", 2), ("z1", 3), ("ay1", 3), ("x2b", 3), ("d1", 3), ("z2", 2), ("z2", 3), ("z3", 2), ("ay2", 3),
-    ("z3", 3), ("d2", 3), ("d4", 2), ("d4", 3), ("d3", 3),
+    ("load", "raw"), ("ox1", "raw"), ("oyB", "raw"), ("od", "raw"), ("oxB", "raw"), ("ay0", "raw"),
+    ("ox2", "raw"), ("coef", 3), ("coef", 2), ("yB2", "raw"), ("coef", 1), ("coef", 0), ("oy", "raw"),
+    ("sum", 3), ("xB2", "raw"), ("sum", 2), ("ay1", "raw"), ("sum", 1), ("mean", 3), ("z0", "raw"),
+    ("x2a", "raw"), ("mean", 2), ("sum", 0), ("mean", 1), ("y2", "raw"), ("rows", 3), ("ox1", 3), ("oyB", 3),
+    ("od", 3), ("oxB", 3), ("ox2", 3), ("ay0", 3), ("oy", 3), ("z1", "raw"), ("d1", "raw"), ("x2b", "raw"),
+    ("mean", 0), ("yB2", 3), ("rows", 2), ("ox1", 2), ("oyB", 2), ("od", 2), ("oxB", 2), ("ox2", 2),
+    ("rows", 1), ("oyB", 1), ("od", 1), ("oxB", 1), ("oy", 2), ("z2", "raw"), ("d2", "raw"), ("ox1", 1),
+    ("xB2", 3), ("yB2", 2), ("yB2", 1), ("x2a", 3), ("oy", 1), ("rows", 0), ("od", 0), ("z0", 3), ("z3", "raw"),
+    ("oy", 0), ("xB2", 1), ("xB2", 2), ("ox1", 0), ("x2a", 2), ("z0", 2), ("y2", 3), ("z1", 3), ("z0", 1),
+    ("y2", 2), ("d4", "raw"), ("x2a", 1), ("y2", 1), ("z1", 2), ("d1", 3), ("x2b", 3), ("y2", 0),
+    ("ay2", "raw"), ("d1", 2), ("z2", 3), ("x2b", 2), ("d1", 1), ("z1", 1), ("x2b", 1), ("d1", 0), ("x2b", 0),
+    ("z2", 2), ("d2", 3), ("z3", 3), ("ay1", 3), ("d2", 2), ("x2a", 0), ("z2", 1), ("ay0", 2), ("d2", 1),
+    ("d3", "raw"), ("ay1", 2), ("z3", 2), ("ay2", 3), ("d4", 3), ("z3", 1), ("d2", 0), ("d4", 2), ("ay2", 2),
+    ("fix", 0), ("d3", 3), ("fix", 1), ("d3", 2), ("d4", 1), ("fix", 2), ("fix", 3),
 ]
 
 
@@ -75,7 +79,7 @@
 
 
 def outer_kernel(local_ref, glob_ref, mom_in, kept_ref, T, new_mom,
-                 lbuf, gbuf, mom, forward, inverse, lhs, coefs, parts, swap_out, swap_in, means,
+                 lbuf, gbuf, mom, steps, forward, inverse, lhs, coefs, parts, swap_out, swap_in, means,
                  load_sem, send_sem, recv_sem):
     x, y, z, c = here()
     all_copies = []
@@ -112,6 +116,11 @@
         pl.semaphore_signal(barrier, inc=1, device_id=peer)
 
     loads = []
+    first = pl.ds(*CHUNKS[0])
+    raw_load = pltpu.make_async_copy(
+        glob_ref.at[first], T.at[0, 0, first], load_sem.at[2 * NQ + 1]
+    )
+    raw_load.start()
     for q, (start, size) in enumerate(CHUNKS):
         rows = pl.ds(start, size)
         pair = [
@@ -123,7 +132,7 @@
         loads.append(pair)
     mom_load = pltpu.make_async_copy(mom_in, mom, load_sem.at[2 * NQ])
     mom_load.start()
-    make_bases(kept_ref, forward, inverse)
+    pl.semaphore_wait(barrier, len(peers))
 
     def zi(k):
         return lax.rem(z + k + 2 * NZ, NZ)
@@ -131,7 +140,12 @@
     def column_group(i):
         return (i % 2) * NZ + i // 2
 
+    ready = []
+
     def coef(q):
+        if not ready:
+            make_bases(kept_ref, forward, inverse)
+            ready.append(q)
         for copy in loads[q]:
             copy.wait()
         start, size = CHUNKS[q]
@@ -145,8 +159,6 @@
         )
         out = both[:, : 4 * KEEP] + both[:, 4 * KEEP :]
         coefs[:, :, rows] = out.astype(jnp.bfloat16).reshape(NZ, 2, size, 4 * KEEP)
-        if q == 0:
-            pl.semaphore_wait(barrier, len(peers))
         return [
             remote(coefs.at[zi(d), :, rows], parts.at[d, :, rows], along[d])
             for d in range(1, NZ)
@@ -172,10 +184,20 @@
             for d in range(1, NZ)
         ]
 
+    def subtract(size, get, put):
+        update = jnp.dot(
+            lhs[: GROUPS * size, : 8 * KEEP], inverse[...], preferred_element_type=jnp.float32
+        )
+        for i in range(GROUPS):
+            cols = pl.ds(column_group(i) * GW, GW)
+            rest = get(cols).astype(jnp.float32) - update[i * size : (i + 1) * size]
+            put(cols, rest.astype(jnp.bfloat16))
+
     def new_rows(q):
         arrive(("mean", q))
-        if q == 0:
+        if not mom_ready:
             mom_load.wait()
+            mom_ready.append(q)
         start, size = CHUNKS[q]
         rows = pl.ds(start, size)
         for i in range(GROUPS):
@@ -184,22 +206,59 @@
             fresh = 0.9 * mom[rows, cols] + avg
             new_mom[rows, cols] = fresh
             step = (avg + 0.9 * fresh).astype(jnp.bfloat16)
-            lhs[pl.ds(i * size, size), : 4 * KEEP] = step
-            lhs[pl.ds(i * size, size), 4 * KEEP : 8 * KEEP] = step
-        update = jnp.dot(
-            lhs[: GROUPS * size, : 8 * KEEP], inverse[...], preferred_element_type=jnp.float32
-        )
-        for i in range(GROUPS):
-            cols = pl.ds(column_group(i) * GW, GW)
-            mine = gbuf[rows, cols].astype(jnp.float32) - update[i * size : (i + 1) * size]
-            T[0, 0, rows, cols] = mine.astype(jnp.bfloat16)
+            if q == 0:
+                steps[0, 0, :, cols] = step
+            else:
+                lhs[pl.ds(i * size, size), : 4 * KEEP] = step
+                lhs[pl.ds(i * size, size), 4 * KEEP : 8 * KEEP] = step
+
+        def put(cols, value):
+            T[0, 0, rows, cols] = value
+
+        if q > 0:
+            subtract(size, lambda cols: gbuf[rows, cols], put)
+        return []
+
+    mom_ready = []
+
+    def load_raw(q):
+        raw_load.wait()
+        return []
+
+    def finish_raw(part):
+        parity = part // 2
+        if part == 0:
+            arrive(*[key for key in flying if key[1] in ("raw", 0) and key[0] not in SHARES])
+            for copy in raw_copies:
+                copy.wait_send()
+        if part == 2:
+            arrive(*[key for key in flying if key[1] in ("raw", 0)])
+        size = CHUNKS[0][1]
+
+        def one(n, carry):
+            slot = (part % 2) * 4 + n
+            for i in range(GROUPS):
+                cols = pl.ds(column_group(i) * 4 * KEEP, 4 * KEEP)
+                step = steps[parity, slot, :, cols]
+                lhs[pl.ds(i * size, size), : 4 * KEEP] = step
+                lhs[pl.ds(i * size, size), 4 * KEEP : 8 * KEEP] = step
+
+            def put(cols, value):
+                T[parity, slot, first, cols] = value
+
+            subtract(size, lambda cols: T[parity, slot, first, cols], put)
+            return carry
+
+        lax.fori_loop(0, 4, one, 0)
         return []
 
     def pass_on(q, name):
         a1, a2, b = SPLIT[q]
         a = a1 + a2
-        rows = pl.ds(*CHUNKS[q])
-        odd = q % 2
+        width = a + NZ * b
+        buf = steps if q == 0 else T
+        rows = pl.ds(0, CHUNKS[0][1]) if q == 0 else first if q == "raw" else pl.ds(*CHUNKS[q])
+        odd = 0 if q == "raw" else q % 2
         p, p0, p1 = pl.ds(0, a1), pl.ds(0, a1 // 2), pl.ds(a1 // 2, a1 // 2)
         s, s0, s1 = pl.ds(a1, a2), pl.ds(a1, a2 // 2), pl.ds(a1 + a2 // 2, a2 // 2)
 
@@ -208,12 +267,12 @@
 
         def send(slot, to_slot, cols, to, landing=None):
             return remote(
-                T.at[0, slot, rows, cols], T.at[0, to_slot, rows, cols], to,
-                None if landing is None else T.at[0, to_slot, rows, landing],
+                buf.at[0, slot, rows, cols], buf.at[0, to_slot, rows, cols], to,
+                None if landing is None else buf.at[0, to_slot, rows, landing],
             )
 
         def share(slot, cols):
-            return [remote(T.at[0, slot, rows, cols], T.at[1, slot, rows, cols], sibling)]
+            return [remote(buf.at[0, slot, rows, cols], buf.at[1, slot, rows, cols], sibling)]
 
         near, away = pl.ds(1, 3), pl.ds(5, 3)
         others = pl.ds(1, 7)
@@ -222,7 +281,7 @@
         if name == "oy":
             return [send(0, 3, p, up), send(0, 1, p, down)]
         if name == "od":
-            return share(0, pl.ds(0, D))
+            return share(0, pl.ds(0, width))
         if name == "y2":
             arrive(("oy", q))
             return [send(3, 2, p0, up), send(1, 2, p1, down)]
@@ -264,7 +323,7 @@
             return [send(near, away, mine, left if odd else right)]
         if name == "d4":
             arrive(("z3", q))
-            return share(others, pl.ds(a, D - a))
+            return share(others, pl.ds(a, width - a))
         hop = int(name[1])
         arrive(*((("xB2", q), ("oxB", q)) if hop == 0 else (("z%d" % (hop - 1), q),)))
         onward = [
@@ -275,15 +334,21 @@
             onward = onward[odd : odd + 1]
         return [send(others, others, cols, to, landing) for cols, to, landing in onward]
 
-    compute = {"coef": coef, "sum": partial_sum, "mean": mean, "rows": new_rows}
+    raw_copies = []
+    compute = {"coef": coef, "sum": partial_sum, "mean": mean, "rows": new_rows,
+               "load": load_raw, "fix": finish_raw}
     for name, q in ORDER:
+        before = len(all_copies)
         if name in compute:
             flying[name, q] = compute[name](q)
         else:
             flying[name, q] = pass_on(q, name)
+        if q == "raw":
+            raw_copies += all_copies[before:]
     arrive(*list(flying))
     for copy in all_copies:
-        copy.wait_send()
+        if not any(copy is other for other in raw_copies):
+            copy.wait_send()
 
 
 def place_kernel(T, mom, params, new_mom, sem):
@@ -322,6 +387,7 @@
             pltpu.VMEM((SHARD, D), bf16),
             pltpu.VMEM((SHARD, D), bf16),
             pltpu.VMEM((SHARD, D // 4), f32),
+            pltpu.VMEM((2, 8, CHUNKS[0][1], D // 4), bf16),
             pltpu.VMEM((GW, 8 * KEEP), bf16),
             pltpu.VMEM((8 * KEEP, GW), bf16),
             pltpu.VMEM((GROUPS * max(size for _, size in CHUNKS), GW), bf16),
@@ -330,7 +396,7 @@
             pltpu.VMEM((2, SHARD, 4 * KEEP), bf16),
             pltpu.VMEM((2, SHARD, 4 * KEEP), bf16),
             pltpu.VMEM((NZ, 2, SHARD, 4 * KEEP), bf16),
-            pltpu.SemaphoreType.DMA((2 * NQ + 1,)),
+            pltpu.SemaphoreType.DMA((2 * NQ + 2,)),
             pltpu.SemaphoreType.DMA((SEMAPHORES,)),
             pltpu.SemaphoreType.DMA((SEMAPHORES,)),
         ],

time: 113 us -> 105 us (0.929)
  Pallas kernels: 112 us -> 105 us
    pallas_call x1, Pallas kernels: 101 us -> 93.3 us  [on_device(): pl.pallas_call(outer_kernel, out_shape=(pltpu.VMEM((2, 8, SHARD, D), bf16...]
where the time goes in v3:
time: 105 us
  Pallas kernels  105 us (100%)
    pallas_call x1, Pallas kernels, on_device(): pl.pallas_call(outer_kernel, out_shape=(pltpu.VMEM((2, 8, SHARD, D), bf16...  93.3 us
    pallas_call x1, Pallas kernels, on_device(): pl.pallas_call(place_kernel, out_shape=(jax.ShapeDtypeStruct((ROWS, D), b...  11.4 us

profile of v3, /device:TPU:1, one launch (start us, length us, event | category | flops | bytes accessed | tf_op | source)
XLA Modules:
  0.0 105.3 jit_solution(8971019282315259517)
XLA Ops:
  0.6 93.3 %shard_map.59 = (bf16[2,8,128,8192]{3,2,1,0:T(8,128)(2,1)S(1)}, f32[128,2048]{1,0:T(8,128)S(1)}) custom-call(bf16[1,128,8192]{2,1,0:T(8,128)(2,1)} %local_ref.1, bf16[128,8192]{1,0:T(8,128)(2,1)} %glob_ref.1, f32[128,2048]{1,0:T(8,128)} %mom_in.1, s32[1,32]{1,0:T(1,128)} %bitcast.1), custom_call_target="tpu_custom_call" | custom-call | tf_op jit(solution)/shard_map/pallas_call | solution.py:381
  93.9 11.4 %shard_map.60 = (bf16[2048,8192]{1,0:T(8,128)(2,1)}, f32[128,2048]{1,0:T(8,128)}) custom-call(bf16[2,8,128,8192]{3,2,1,0:T(8,128)(2,1)S(1)} %get-tuple-element.4.T, f32[128,2048]{1,0:T(8,128)S(1)} %get-tuple-element.5.mom), custom_call_target="tpu_custom_call" | custom-call | tf_op jit(solution)/shard_map/pallas_call | solution.py:407

commit v4 on v3

--- a/solution.py
+++ b/solution.py
@@ -132,6 +132,7 @@
         loads.append(pair)
     mom_load = pltpu.make_async_copy(mom_in, mom, load_sem.at[2 * NQ])
     mom_load.start()
+    make_bases(kept_ref, forward, inverse)
     pl.semaphore_wait(barrier, len(peers))
 
     def zi(k):
@@ -140,12 +141,7 @@
     def column_group(i):
         return (i % 2) * NZ + i // 2
 
-    ready = []
-
     def coef(q):
-        if not ready:
-            make_bases(kept_ref, forward, inverse)
-            ready.append(q)
         for copy in loads[q]:
             copy.wait()
         start, size = CHUNKS[q]

time: 105 us -> 105 us (level)
  no operation moved by 1% of the time
where the time goes in v4:
time: 105 us
  Pallas kernels  105 us (100%)
    pallas_call x1, Pallas kernels, on_device(): pl.pallas_call(outer_kernel, out_shape=(pltpu.VMEM((2, 8, SHARD, D), bf16...  93.3 us
    pallas_call x1, Pallas kernels, on_device(): pl.pallas_call(place_kernel, out_shape=(jax.ShapeDtypeStruct((ROWS, D), b...  11.4 us

profile of v4, /device:TPU:1, one launch (start us, length us, event | category | flops | bytes accessed | tf_op | source)
XLA Modules:
  0.0 105.3 jit_solution(17052886845097374568)
XLA Ops:
  0.6 93.3 %shard_map.59 = (bf16[2,8,128,8192]{3,2,1,0:T(8,128)(2,1)S(1)}, f32[128,2048]{1,0:T(8,128)S(1)}) custom-call(bf16[1,128,8192]{2,1,0:T(8,128)(2,1)} %local_ref.1, bf16[128,8192]{1,0:T(8,128)(2,1)} %glob_ref.1, f32[128,2048]{1,0:T(8,128)} %mom_in.1, s32[1,32]{1,0:T(1,128)} %bitcast.1), custom_call_target="tpu_custom_call" | custom-call | tf_op jit(solution)/shard_map/pallas_call | solution.py:377
  93.9 11.4 %shard_map.60 = (bf16[2048,8192]{1,0:T(8,128)(2,1)}, f32[128,2048]{1,0:T(8,128)}) custom-call(bf16[2,8,128,8192]{3,2,1,0:T(8,128)(2,1)S(1)} %get-tuple-element.4.T, f32[128,2048]{1,0:T(8,128)S(1)} %get-tuple-element.5.mom), custom_call_target="tpu_custom_call" | custom-call | tf_op jit(solution)/shard_map/pallas_call | solution.py:403

commit v5 on v4

--- a/solution.py
+++ b/solution.py
@@ -14,6 +14,7 @@
 REPLICAS = 16
 GROUPS = 16
 GW = D // GROUPS
+PIECES = 4
 VMEM = 24 << 20
 CHUNKS = [(0, 48), (48, 16), (64, 32), (96, 32)]
 NQ = len(CHUNKS)
@@ -349,7 +350,7 @@
 
 def place_kernel(T, mom, params, new_mom, sem):
     x, y, z, c = here()
-    copies = [pltpu.make_async_copy(mom, new_mom, sem.at[16])]
+    copies = []
     for p in range(2):
         for dy in range(4):
             for dx in range(2):
@@ -357,12 +358,16 @@
                 shard = (
                     lax.rem(y + dy, NY) * 4 + lax.rem(x + dx, 2) * 2 + lax.rem(c + p, 2)
                 )
-                rows = pl.ds(pl.multiple_of(shard * SHARD, SHARD), SHARD)
-                copies.append(
-                    pltpu.make_async_copy(
-                        T.at[p, slot], params.at[rows], sem.at[p * 8 + slot]
+                for part in range(PIECES):
+                    size = SHARD // PIECES
+                    rows = pl.ds(pl.multiple_of(shard * SHARD + part * size, size), size)
+                    copies.append(
+                        pltpu.make_async_copy(
+                            T.at[p, slot, pl.ds(part * size, size)], params.at[rows],
+                            sem.at[len(copies)],
+                        )
                     )
-                )
+    copies.append(pltpu.make_async_copy(mom, new_mom, sem.at[len(copies)]))
     for copy in copies:
         copy.start()
     for copy in copies:
@@ -408,7 +413,7 @@
         ),
         in_specs=[in_vmem, in_vmem],
         out_specs=(anywhere, anywhere),
-        scratch_shapes=[pltpu.SemaphoreType.DMA((17,))],
+        scratch_shapes=[pltpu.SemaphoreType.DMA((16 * PIECES + 1,))],
         compiler_params=pltpu.CompilerParams(vmem_limit_bytes=VMEM),
     )(
         pltpu.with_memory_space_constraint(T, pltpu.VMEM),

time: 105 us -> 106 us (level)
  no operation moved by 1% of the time
where the time goes in v5:
time: 106 us
  Pallas kernels  105 us (99%)
    pallas_call x1, Pallas kernels, on_device(): pl.pallas_call(outer_kernel, out_shape=(pltpu.VMEM((2, 8, SHARD, D), bf16...  93.3 us
    pallas_call x1, Pallas kernels, on_device(): pl.pallas_call(place_kernel, out_shape=(jax.ShapeDtypeStruct((ROWS, D), b...  11.8 us

profile of v5, /device:TPU:1, one launch (start us, length us, event | category | flops | bytes accessed | tf_op | source)
XLA Modules:
  0.0 105.7 jit_solution(4385150092403157662)
XLA Ops:
  0.6 93.3 %shard_map.59 = (bf16[2,8,128,8192]{3,2,1,0:T(8,128)(2,1)S(1)}, f32[128,2048]{1,0:T(8,128)S(1)}) custom-call(bf16[1,128,8192]{2,1,0:T(8,128)(2,1)} %local_ref.1, bf16[128,8192]{1,0:T(8,128)(2,1)} %glob_ref.1, f32[128,2048]{1,0:T(8,128)} %mom_in.1, s32[1,32]{1,0:T(1,128)} %bitcast.1), custom_call_target="tpu_custom_call" | custom-call | tf_op jit(solution)/shard_map/pallas_call | solution.py:382
  93.9 11.8 %shard_map.60 = (bf16[2048,8192]{1,0:T(8,128)(2,1)}, f32[128,2048]{1,0:T(8,128)}) custom-call(bf16[2,8,128,8192]{3,2,1,0:T(8,128)(2,1)S(1)} %get-tuple-element.4.T, f32[128,2048]{1,0:T(8,128)S(1)} %get-tuple-element.5.mom), custom_call_target="tpu_custom_call" | custom-call | tf_op jit(solution)/shard_map/pallas_call | solution.py:408
